TPU v7x, 32 devices: a whole 2x2x4 slice. The times are simulated.
32 devices in a mesh: stn: 8 (over z, y), grid: 4 (over x, core).
Axes of the slice: x: 2, y: 2, z: 4, core: 2. Of those that a mesh axis runs over, the one named last changes fastest.
Arguments:
- voltages: bfloat16 [512, 2, 12288], P('stn', None, 'grid'), may hold values from -6 to 6
- pfb_coeffs: float32 [16, 48], replicated, may hold values from -1.5 to 1.5
- station_offsets: int32 [2, 512], replicated, may hold values from 0 to 4
- tile_cells: int32 [24, 2, 136], P('stn'), may hold values from 0 to 127, as said below
- kernel_table: float32 [8, 7], replicated, may hold values from 0.2 to 1
Outputs:
- uv_grid: float32 [128, 24, 256], P('grid', 'stn')
Inputs may be any that keep to these rules, and one draw needn't show every extreme that they name: tile_cells[c, 0, k] lies in one of the strips of 32 rows; in every channel at most 68 baseline tiles have their base row in the same strip, and one strip holds exactly 68. A base row in the last strip and every base column are at most 112.
All inputs are finite; a program needn't handle non-finite values.
Results may differ from a plain program's by a relative error of at most 0.0065.
Values may be sent and summed in bfloat16 or wider, within the bound.
A program may use at most 128 MiB of HBM per device.

v0:
```python
import math

import jax
import jax.numpy as jnp
import numpy as np
from jax import lax
from jax.sharding import PartitionSpec as P

TILE = 32
PATCH = 16
SPREAD = 5
UV = 128


highest = lax.Precision.HIGHEST


def shifted(block, axis, distance):
    devices = range(lax.axis_size(axis))
    route = [(i - distance, i) for i in devices if i - distance in devices]
    return lax.ppermute(block, axis, route)


def dft_table(frame_len):
    chan_count = frame_len // 2
    sample_line = jnp.arange(frame_len, dtype=jnp.int32)[:, None]
    chan_line = jnp.arange(chan_count, dtype=jnp.int32)[None, :]
    angles = (sample_line * chan_line % frame_len).astype(jnp.float32) * (2.0 * math.pi / frame_len)
    norm_factor = 1.0 / math.sqrt(frame_len)
    twiddle = jnp.stack([jnp.cos(angles) * norm_factor, -jnp.sin(angles) * norm_factor], axis=2)
    return twiddle.reshape(frame_len, 2 * chan_count).astype(jnp.bfloat16)


CLASSES = 32
high = lax.Precision.HIGH


def fused_filter(coeffs, twiddle, step):
    taps, frame_len = coeffs.shape
    flat = coeffs.reshape(-1)
    columns = [
        jnp.pad(flat, (frame_len * (f + 1), frame_len * (step - 1 - f))) for f in range(step)
    ]
    shifted_coeffs = jnp.stack(columns, axis=0)
    spread = np.kron(np.ones((1, frame_len), np.float32), np.eye(step, dtype=np.float32))
    wide = jnp.einsum("fm,fn->mn", shifted_coeffs, jnp.asarray(spread), precision=highest)
    tiled = jnp.tile(jnp.repeat(twiddle.astype(jnp.float32), step, axis=1), (step + taps, 1))
    return (wide * tiled).astype(jnp.bfloat16)

def separation_table(frequency, divisor, kernel_table):
    over_count = kernel_table.shape[0]
    separation = jnp.arange(2 * SPREAD - 1, dtype=jnp.int32)
    scaled = separation * frequency
    cell_index = scaled // divisor
    fine_index = scaled % divisor * over_count // divisor
    choose = (fine_index[:, None] == jnp.arange(over_count, dtype=jnp.int32)[None, :]).astype(
        jnp.float32
    )
    tap_values = jnp.dot(choose, kernel_table, precision=highest)
    place_rel = jnp.arange(PATCH, dtype=jnp.int32)[None, :] - cell_index[:, None]
    weights = jnp.zeros(place_rel.shape, jnp.float32)
    for tap_index in range(kernel_table.shape[1]):
        weights = weights + tap_values[:, tap_index : tap_index + 1] * (
            place_rel == tap_index
        ).astype(jnp.float32)
    return weights


def joint_weights(frequencies, divisor, kernel_table):
    class_line = np.arange(CLASSES)
    class_u = np.minimum(class_line // SPREAD, SPREAD - 1)
    class_v = class_line % SPREAD
    sep_line = np.arange(2 * SPREAD - 1)
    pick_u = (class_u[:, None] - class_u[None, :] + SPREAD - 1).reshape(-1, 1) == sep_line
    pick_v = (class_v[:, None] - class_v[None, :] + SPREAD - 1).reshape(-1, 1) == sep_line
    weights = jnp.stack([separation_table(f, divisor, kernel_table) for f in frequencies])
    over_r = np.kron(np.eye(PATCH), np.ones((1, PATCH))).astype(np.float32)
    over_t = np.kron(np.ones((1, PATCH)), np.eye(PATCH)).astype(np.float32)
    wide_u = jnp.einsum("czr,rm->czm", weights, jnp.asarray(over_r), precision=highest)
    wide_v = jnp.einsum("czr,rm->czm", weights, jnp.asarray(over_t), precision=highest)
    full_u = jnp.einsum("qz,czm->cqm", jnp.asarray(pick_u.astype(np.float32)), wide_u, precision=highest)
    full_v = jnp.einsum("qz,czm->cqm", jnp.asarray(pick_v.astype(np.float32)), wide_v, precision=highest)
    return full_u * full_v


def body(voltages, pfb_coeffs, station_offsets, tile_cells, kernel_table):
    stn_local, pol_count, samples = voltages.shape
    tap_count, frame_len = pfb_coeffs.shape
    spec_count = samples // frame_len
    step = 128 // math.gcd(128, frame_len)
    chunks = spec_count // step
    flat = voltages.reshape(stn_local * pol_count, samples)
    earlier = shifted(flat[:, samples - tap_count * frame_len :], "grid", 1)
    extended = jnp.concatenate([earlier, flat], axis=1)
    width = step * frame_len
    reach = (step + tap_count) * frame_len
    blocks = jnp.stack(
        [extended[:, c * width : c * width + reach] for c in range(chunks)], axis=1
    )
    matrix = fused_filter(pfb_coeffs, dft_table(frame_len), step)
    spectra = jnp.einsum(
        "rcm,mn->nrc", blocks, matrix, preferred_element_type=jnp.float32
    ).astype(jnp.bfloat16)
    spectra = spectra.reshape(frame_len // 2, 2, step, stn_local, pol_count * chunks)
    spectra = jnp.transpose(spectra, (0, 1, 3, 2, 4)).reshape(
        frame_len // 2, 2, stn_local, step * pol_count * chunks
    )
    turned = lax.all_to_all(spectra, "stn", split_axis=0, concat_axis=2, tiled=True)
    ch_dev, _, stations, depth = turned.shape
    tiles = stations // TILE
    divisor = frame_len - 1
    first_chan = lax.axis_index("stn") * ch_dev + frame_len // 2
    norm_factor = 1.0 / (pol_count * spec_count * lax.axis_size("grid"))

    classes = (station_offsets[0] * SPREAD + station_offsets[1]).reshape(tiles, TILE)
    hot = classes[:, :, None] == jnp.arange(CLASSES, dtype=jnp.int32)
    hot_low = hot.astype(jnp.bfloat16)
    hot_full = hot.astype(jnp.float32)
    tiled = turned.reshape(ch_dev, 2, tiles, TILE, depth)
    summed = jnp.einsum(
        "aiq,ceaik->ceaqk", hot_low, tiled, preferred_element_type=jnp.float32
    ).astype(jnp.bfloat16)

    def stacked(z):
        real_part, imag_part = z[:, 0], z[:, 1]
        partner = jnp.concatenate([real_part, imag_part], axis=-1)
        turned_partner = jnp.concatenate([imag_part, -real_part], axis=-1)
        return jnp.stack([partner, turned_partner], axis=1), partner

    left, right = stacked(summed)
    cross = jnp.einsum("ceaqk,cbsk->ceabqs", left, right, preferred_element_type=jnp.float32)
    joint = joint_weights([first_chan + i for i in range(ch_dev)], divisor, kernel_table)
    joint = joint * norm_factor
    patch = jnp.einsum(
        "ceabm,cmn->ceabn",
        cross.reshape(ch_dev, 2, tiles, tiles, CLASSES * CLASSES),
        joint,
        precision=high,
    )
    own_left, own_right = stacked(tiled)
    own = jnp.einsum("ceaik,cajk->ceaij", own_left, own_right, preferred_element_type=jnp.float32)
    line = np.arange(TILE)
    own = jnp.where(jnp.asarray(line[:, None] < line[None, :]), own, 0.0)
    own = jnp.einsum("aiq,ceaij->ceaqj", hot_full, own, precision=high)
    own = jnp.einsum("ceaqj,ajs->ceaqs", own, hot_full, precision=high)
    own_patch = jnp.einsum(
        "ceam,cmn->cean", own.reshape(ch_dev, 2, tiles, CLASSES * CLASSES), joint, precision=high
    )
    same = np.eye(tiles, dtype=bool)[:, :, None]
    patch = jnp.where(jnp.asarray(same), own_patch[:, :, :, None, :], patch)

    pair_first, pair_second = np.triu_indices(tiles)
    select = np.zeros((pair_first.size, tiles * tiles), np.float32)
    select[np.arange(pair_first.size), pair_first * tiles + pair_second] = 1.0
    missing = (1.0 - select.sum(axis=0)).astype(np.int32) * 4096
    cells = jnp.einsum(
        "cxk,kp->cxp", tile_cells.astype(jnp.float32), jnp.asarray(select), precision=highest
    )
    cells = jnp.round(cells).astype(jnp.int32) + jnp.asarray(missing)
    patch = patch.reshape(ch_dev, 2, tiles * tiles, PATCH, PATCH)
    patch_line = jnp.arange(PATCH, dtype=jnp.int32)
    target = cells[..., None] + patch_line
    spots = (target[..., None] == jnp.arange(UV, dtype=jnp.int32)).astype(jnp.float32)
    rows, cols = spots[:, 0], spots[:, 1]
    spread_cols = jnp.einsum("cekrt,cktw->ckrew", patch, cols, precision=high)
    planes = jnp.einsum("ckru,ckrew->ucew", rows, spread_cols, precision=high)
    planes = planes.reshape(UV, ch_dev, 2 * UV)
    return lax.psum_scatter(planes, "grid", scatter_dimension=0, tiled=True)


def solution(mesh):
    placed = (P("stn", None, "grid"), P(), P(), P("stn", None, None), P())
    return jax.shard_map(
        body, mesh=mesh, in_specs=placed, out_specs=P("grid", "stn", None), check_vma=False
    )
```

profile of v0, /device:TPU:0, one launch (start us, length us, event | category | flops | bytes accessed | tf_op | source)
XLA Modules:
  0.0 228.6 jit_solution(5774973549644276165)
XLA Ops:
  6.5 2.3 %reshape.1055 = bf16[128,3072]{1,0:T(8,128)(2,1)S(1)} reshape(bf16[64,2,3072]{2,1,0:T(2,128)(2,1)} %param.14) | data formatting | bytes 1572864 | tf_op jit(solution)/shard_map/reshape | solution.py:92
  8.9 2.4 %collective-permute-start = (bf16[128,768]{1,0:T(8,128)(2,1)S(1)}, bf16[128,768]{1,0:T(8,128)(2,1)S(1)}, u32[]{:S(2)}, u32[]{:S(2)}) collective-permute-start(bf16[128,768]{1,0:T(8,128)(2,1)S(1)} %slice.161), channel_id=1, source_target_pairs={{0,1},{1,2},{2,3},{4,5},{5,6},{6,7},{8,9},{9,10},{10,11},{12,13},{... | collective-permute-start | bytes 589832 | tf_op jit(solution)/shard_map/ppermute | solution.py:21
  11.3 0.1 multiply_convert_fusion
  11.4 0.1 reshape.1054
  11.5 0.1 fusion.98
  11.6 0.1 copy.101
  11.8 0.2 fusion.82
  12.0 0.2 fusion.81
  12.3 0.2 fusion.80
  12.5 0.0 copy-done.12
  12.5 0.1 select_add_fusion
  12.6 0.1 select_add_fusion.1
  12.7 0.0 copy-start.14
  12.7 0.0 copy-start.15
  12.7 0.0 copy-start.16
  12.7 0.0 copy-start.17
  12.7 0.0 copy-start.18
  12.7 0.0 copy-start.19
  12.7 0.0 copy-start.20
  12.8 0.0 copy-start.21
  12.8 0.1 select_add_fusion.2
  12.9 0.2 fusion.53
  13.1 0.0 copy-start.8
  13.1 4.3 %fusion.99 = f32[3,256,1024]{2,1,0:T(8,128)} fusion(f32[3,9,256]{2,1,0:T(8,128)S(1)} %fusion.53, f32[1024,9,1]{0,1,2:T(8,128)S(1)} %copy-done.7), kind=kOutput, calls=%fused_computation.178 | convolution fusion | flops 84934656 | bytes 3210240 | tf_op jit(solution)/shard_map/qz,czm->cqm/dot_general | solution.py:81
  17.4 0.2 fusion.29
  17.7 1.3 fusion.8
  19.0 0.2 fusion.52
  19.2 0.1 constant_dynamic-update-slice_fusion
  19.5 1.2 convolution_convert_fusion.1
  20.8 0.5 copy.103
  21.3 15.6 %reshape.1056 = bf16[24,2,8,64,16]{2,1,0,4,3:T(2,128)(2,1)} reshape(bf16[384,128,8]{0,2,1:T(8,128)(2,1)S(1)} %copy.103) | data formatting | bytes 1572864 | tf_op jit(solution)/shard_map/reshape | solution.py:104
  37.0 30.5 %copy.104 = bf16[24,2,64,8,16]{2,4,3,1,0:T(8,128)(2,1)S(1)} copy(bf16[24,2,64,8,16]{3,1,0,4,2:T(2,128)(2,1)} %bitcast.218) | data formatting | bytes 1572864 | tf_op jit(solution)/shard_map/transpose | solution.py:105
  67.5 1.4 copy.105
  68.9 6.8 %all-to-all-start = ((bf16[24,2,64,128]{3,2,1,0:T(8,128)(2,1)}), bf16[24,2,64,128]{3,2,1,0:T(8,128)(2,1)}, u32[]{:S(2)}, u32[]{:S(2)}) async-start(bf16[24,2,64,128]{3,2,1,0:T(8,128)(2,1)} %copy.105), calls=%async_computation | async-start | bytes 1572864 | tf_op jit(solution)/shard_map/all_to_all | solution.py:108
  75.7 0.2 reduce-scatter.2.cloned.1.call-start
  76.0 0.1 add.327
  76.1 0.3 iota_add_fusion
  76.3 4.7 %multiply_multiply_fusion = f32[3,256,1024]{2,1,0:T(8,128)S(1)} fusion(f32[3,256,1024]{2,1,0:T(8,128)} %fusion.99, f32[3,9,256]{2,1,0:T(8,128)S(1)} %fusion.52, f32[1024,9,1]{0,1,2:T(8,128)S(1)} %copy-done.6), kind=kOutput, calls=%fused_computation.12 | convolution fusion | flops 86507520 | bytes 6355968 | tf_op jit(solution)/shard_map/qz,czm->cqm/dot_general | solution.py:82
  81.1 5.4 %iota_compare_fusion = pred[3,2,256,16,128]{4,3,2,0,1:T(8,128)(4,1)} fusion(s32[3,2,256,16]{3,2,0,1:T(8,128)S(1)} %iota_add_fusion), kind=kLoop, calls=%fused_computation.4 | loop fusion | flops 3145728 | bytes 3244032 | tf_op jit(solution)/shard_map/eq | solution.py:163
  86.5 10.8 %all-to-all-done = bf16[24,2,64,128]{3,2,1,0:T(8,128)(2,1)} async-done(((bf16[24,2,64,128]{3,2,1,0:T(8,128)(2,1)}), bf16[24,2,64,128]{3,2,1,0:T(8,128)(2,1)}, u32[]{:S(2)}, u32[]{:S(2)}) %all-to-all-start) | async-done | bytes 786464 | tf_op jit(solution)/shard_map/all_to_all | solution.py:108
  97.3 1.2 copy.106
  98.5 0.4 fusion.26
  98.9 0.1 slice_bitcast_fusion.5
  98.9 0.1 fusion.97
  99.0 1.0 slice_bitcast_fusion.7
  100.0 0.1 fusion.96
  100.0 0.3 fusion.34
  100.3 10.1 %convolution_bitcast_fusion = f32[3,2,16,16,32,32]{4,5,2,1,3,0:T(8,128)} fusion(bf16[3,16,32,256,1,1]{3,2,0,1,5,4:T(8,128)(2,1)S(1)} %get-tuple-element.7, bf16[3,1,16,32,256]{4,3,0,2,1:T(8,128)(2,1)S(1)} %get-tuple-element.13, bf16[3,1,16,32,256]{4,3,0,2,1:T(8,128)(2,1)S(1)} %get-tuple-element.8), kind=kOutput, calls=%fused_computation.5 | convolution fusion | flops 806092800 | bytes 8650752 | tf_op jit(solution)/shard_map/ceaqk,cbsk->ceabqs/dot_general | solution.py:131
  110.4 24.9 %copy.118 = f32[3,2,16,16,32,32]{5,4,3,2,1,0:T(8,128)} copy(f32[3,2,16,16,32,32]{4,5,2,1,3,0:T(8,128)} %convolution_bitcast_fusion) | data formatting | bytes 12582912 | tf_op jit(solution)/shard_map/ceaqk,cbsk->ceabqs/transpose | solution.py:131
  135.3 19.9 %reshape.1060 = f32[3,2,16,16,1024]{4,3,2,1,0:T(8,128)} reshape(f32[3,2,16,16,32,32]{5,4,3,2,1,0:T(8,128)} %copy.118) | data formatting | bytes 12582912 | tf_op jit(solution)/shard_map/reshape | solution.py:136
  155.3 1.6 fusion.36
  156.9 1.3 bitcast_select_fusion
  158.2 0.6 fusion.16
  158.8 1.7 fusion.18
  160.6 3.0 %copy.113 = f32[3,2,16,32,32]{4,3,2,1,0:T(8,128)} copy(f32[3,2,16,32,32]{3,4,1,0,2:T(8,128)} %fusion.18) | data formatting | bytes 786432 | tf_op jit(solution)/shard_map/ceaqj,ajs->ceaqs/transpose | solution.py:145
  163.6 2.1 reshape.1059
  165.7 1.5 fusion.6
  167.3 6.8 %fusion.23 = f32[3,2,16,16,256]{4,3,2,1,0:T(8,128)} fusion(f32[3,2,16,16,1024]{4,3,2,1,0:T(8,128)} %reshape.1060, f32[3,256,1024]{2,1,0:T(8,128)S(1)} %multiply_multiply_fusion, f32[3,2,16,256]{3,2,1,0:T(8,128)S(1)} %fusion.6, pred[16,16]{1,0:T(8,128)(4,1)S(1)} %copy-done.11), kind=kOutput, calls=%fused_computation.34 | convolution fusion | flops 2416312320 | bytes 11108608 | tf_op jit(solution)/shard_map/ceabm,cmn->ceabn/dot_general | solution.py:134
  174.1 8.4 %reshape.1061 = f32[3,2,256,16,16]{4,3,2,1,0:T(8,128)} reshape(f32[3,2,16,16,256]{4,3,2,1,0:T(8,128)} %fusion.23) | data formatting | bytes 3145728 | tf_op jit(solution)/shard_map/reshape | solution.py:160
  182.5 9.3 %fusion.2 = f32[3,256,128,2,16]{2,4,3,1,0:T(8,128)} fusion(f32[3,2,256,16,16]{4,3,2,1,0:T(8,128)} %reshape.1061, pred[3,2,256,16,128]{4,3,2,0,1:T(8,128)(4,1)S(1)} %copy-done.2), kind=kOutput, calls=%fused_computation.2 | convolution fusion | flops 301989888 | bytes 15728640 | tf_op jit(solution)/shard_map/cekrt,cktw->ckrew/dot_general | solution.py:165
  191.8 9.8 %fusion = f32[3,2,128,128,1]{3,2,1,4,0:T(8,128)S(1)} fusion(f32[3,256,128,2,16]{2,4,3,1,0:T(8,128)} %fusion.2, pred[3,2,256,16,128]{4,3,2,0,1:T(8,128)(4,1)S(1)} %copy-done.2), kind=kOutput, calls=%fused_computation | convolution fusion | flops 2415919104 | bytes 14548992 | tf_op jit(solution)/shard_map/ckru,ckrew->ucew/dot_general | solution.py:166
  201.7 0.9 copy.121
  202.6 0.0 reduce-scatter.2.cloned.1.call-update
  202.6 19.1 %reduce-scatter.2.cloned.1.call-done = f32[32,3,256]{2,0,1:T(8,128)} async-done(((f32[128,3,256]{2,0,1:T(8,128)}), f32[32,3,256]{2,0,1:T(8,128)}) %reduce-scatter.2.cloned.1.call-update) | async-done | bytes 98320 | tf_op jit(solution)/shard_map/reduce_scatter | solution.py:168
  (60 shorter events, 0.6 us)
Async XLA Ops:
  6.5 5.2 %copy-start = (f32[8,7]{1,0:T(8,128)S(1)}, f32[8,7]{1,0:T(8,128)}, u32[]{:S(2)}) copy-start(f32[8,7]{1,0:T(8,128)} %param.18) | copy-start | bytes 676
  6.5 6.3 %copy-start.9 = (f32[16,256,1]{1,0,2:T(8,128)S(1)}, f32[16,256,1]{1,0,2:T(8,128)}, u32[]{:S(2)}) copy-start(f32[16,256,1]{1,0,2:T(8,128)} %constant.175) | copy-start | bytes 49156
  6.5 6.5 %copy-start.7 = (f32[1024,9,1]{0,1,2:T(8,128)S(1)}, f32[1024,9,1]{0,1,2:T(8,128)}, u32[]{:S(2)}) copy-start(f32[1024,9,1]{0,1,2:T(8,128)} %constant.176) | copy-start | bytes 110596
  6.5 4.8 %copy-start.10 = (f32[16,48]{1,0:T(8,128)S(1)}, f32[16,48]{1,0:T(8,128)}, u32[]{:S(2)}) copy-start(f32[16,48]{1,0:T(8,128)} %param.15) | copy-start | bytes 9220
  6.5 5.9 %copy-start.12 = (s32[3,2,136]{2,1,0:T(2,128)S(1)}, s32[3,2,136]{2,1,0:T(2,128)}, u32[]{:S(2)}) copy-start(s32[3,2,136]{2,1,0:T(2,128)} %param.17) | copy-start | bytes 9796
  8.9 10.2 %collective-permute-start = (bf16[128,768]{1,0:T(8,128)(2,1)S(1)}, bf16[128,768]{1,0:T(8,128)(2,1)S(1)}, u32[]{:S(2)}, u32[]{:S(2)}) collective-permute-start(bf16[128,768]{1,0:T(8,128)(2,1)S(1)} %slice.161), channel_id=1, source_target_pairs={{0,1},{1,2},{2,3},{4,5},{5,6},{6,7},{8,9},{9,10},{10,11},{12,13},{... | collective-permute-start | bytes 589832 | tf_op jit(solution)/shard_map/ppermute | solution.py:21
  12.2 5.2 %copy-start.5 = (f32[136,256,1]{1,0,2:T(8,128)S(1)}, f32[136,256,1]{1,0,2:T(8,128)}, u32[]{:S(2)}) copy-start(f32[136,256,1]{1,0,2:T(8,128)} %constant.174) | copy-start | bytes 417796
  12.2 5.2 %copy-start.22 = (s32[256]{0:T(256)S(1)}, s32[256]{0:T(256)}, u32[]{:S(2)}) copy-start(s32[256]{0:T(256)} %constant.139.clone) | copy-start | bytes 3076
  12.7 4.9 %copy-start.14 = (f32[384]{0:T(512)S(1)}, f32[384]{0:T(512)}, u32[]{:S(2)}) copy-start(f32[384]{0:T(512)} %constant.173) | copy-start | bytes 4612
  12.7 4.9 %copy-start.15 = (f32[384]{0:T(512)S(1)}, f32[384]{0:T(512)}, u32[]{:S(2)}) copy-start(f32[384]{0:T(512)} %constant.171) | copy-start | bytes 4612
  12.7 4.9 %copy-start.16 = (f32[384]{0:T(512)S(1)}, f32[384]{0:T(512)}, u32[]{:S(2)}) copy-start(f32[384]{0:T(512)} %constant.169) | copy-start | bytes 4612
  12.7 4.9 %copy-start.17 = (f32[384]{0:T(512)S(1)}, f32[384]{0:T(512)}, u32[]{:S(2)}) copy-start(f32[384]{0:T(512)} %constant.167) | copy-start | bytes 4612
  12.7 4.9 %copy-start.18 = (f32[384]{0:T(512)S(1)}, f32[384]{0:T(512)}, u32[]{:S(2)}) copy-start(f32[384]{0:T(512)} %constant.165) | copy-start | bytes 4612
  12.7 4.9 %copy-start.19 = (f32[384]{0:T(512)S(1)}, f32[384]{0:T(512)}, u32[]{:S(2)}) copy-start(f32[384]{0:T(512)} %constant.163) | copy-start | bytes 4612
  12.7 4.9 %copy-start.20 = (f32[384]{0:T(512)S(1)}, f32[384]{0:T(512)}, u32[]{:S(2)}) copy-start(f32[384]{0:T(512)} %constant.161) | copy-start | bytes 4612
  12.8 4.9 %copy-start.21 = (f32[384]{0:T(512)S(1)}, f32[384]{0:T(512)}, u32[]{:S(2)}) copy-start(f32[384]{0:T(512)} %constant.159) | copy-start | bytes 4612
  13.1 5.9 %copy-start.8 = (f32[16,256,1]{1,0,2:T(8,128)S(1)}, f32[16,256,1]{1,0,2:T(8,128)}, u32[]{:S(2)}) copy-start(f32[16,256,1]{1,0,2:T(8,128)} %constant.177) | copy-start | bytes 49156
  67.5 8.4 %copy-start.13 = (s32[2,512]{1,0:T(2,128)S(1)}, s32[2,512]{1,0:T(2,128)}, u32[]{:S(2)}) copy-start(s32[2,512]{1,0:T(2,128)} %param.16) | copy-start | bytes 12292
  68.9 7.4 %copy-start.6 = (f32[1024,9,1]{0,1,2:T(8,128)S(1)}, f32[1024,9,1]{0,1,2:T(8,128)}, u32[]{:S(2)}) copy-start(f32[1024,9,1]{0,1,2:T(8,128)} %constant.178) | copy-start | bytes 110596
  68.9 28.4 %all-to-all-start = ((bf16[24,2,64,128]{3,2,1,0:T(8,128)(2,1)}), bf16[24,2,64,128]{3,2,1,0:T(8,128)(2,1)}, u32[]{:S(2)}, u32[]{:S(2)}) async-start(bf16[24,2,64,128]{3,2,1,0:T(8,128)(2,1)} %copy.105), calls=%async_computation | async-start | bytes 1572864 | tf_op jit(solution)/shard_map/all_to_all | solution.py:108
  75.7 146.0 %reduce-scatter.2.cloned.1.call-start = ((), (), s32[]{:S(2)}) async-start(), calls=%async_computation.2 | async-start | bytes 491520 | tf_op jit(solution)/shard_map/reduce_scatter | solution.py:168
  155.3 1.6 copy-start.3
  155.3 1.6 copy-start.4
  155.3 1.7 copy-start.23
  165.7 1.6 copy-start.11
  174.1 8.4 %copy-start.2 = (pred[3,2,256,16,128]{4,3,2,0,1:T(8,128)(4,1)S(1)}, pred[3,2,256,16,128]{4,3,2,0,1:T(8,128)(4,1)}, u32[]{:S(2)}) copy-start(pred[3,2,256,16,128]{4,3,2,0,1:T(8,128)(4,1)} %iota_compare_fusion) | copy-start | bytes 9437188
  191.8 29.9 %copy-start.1 = (f32[8,7]{1,0:T(8,128)S(1)}, f32[8,7]{1,0:T(8,128)}, u32[]{:S(2)}) copy-start(f32[8,7]{1,0:T(8,128)} %param.18) | copy-start | bytes 676
Sparse Core Ops, SparseCore 0:
  202.7 18.9 reduce-scatter.1
where the time goes:
time: 230 us; the launch traced here: 229 us
  local copies, waits for them, and re-layouts  113 us (49%)
  matrix products  53 us (23%)
  waiting for transfers between devices  30 us (13%)
  between operations  14 us (6%)
  other arithmetic  9.47 us (4%)
  starting transfers between devices  9.38 us (4%)
    transpose x1, local copies, waits for them, and re-layouts, body(): jnp.transpose(spectra, (0, 1, 3, 2, 4))  30.5 us
    transpose x1, local copies, waits for them, and re-layouts, body(): jnp.einsum('ceaqk,cbsk->ceabqs', left, right, preferred_element_type=jnp....  24.9 us
    reshape x1, local copies, waits for them, and re-layouts, body(): cross.reshape(ch_dev, 2, tiles, tiles, CLASSES * CLASSES)  19.9 us
    reduce_scatter x1, waiting for transfers between devices, body(): return lax.psum_scatter(planes, 'grid', scatter_dimension=0, tiled=True)  19.1 us
    reshape x1, local copies, waits for them, and re-layouts, body(): spectra.reshape(frame_len // 2, 2, step, stn_local, pol_count * chunks)  15.6 us
    all_to_all x1, waiting for transfers between devices, body(): lax.all_to_all(spectra, 'stn', split_axis=0, concat_axis=2, tiled=True)  10.8 us
    dot_general x1, matrix products, body(): jnp.einsum('ceaqk,cbsk->ceabqs', left, right, preferred_element_type=jnp....  10.1 us
    dot_general x1, matrix products, body(): planes = jnp.einsum('ckru,ckrew->ucew', rows, spread_cols, precision=high)  9.85 us
  transfers between devices with their start and end apart: 3, of which 2 were waited for; matrix products, arithmetic and copies ran while one was open for 8% of the time, Pallas kernels for 0%

commit v1 on v0

--- a/solution.py
+++ b/solution.py
@@ -71,8 +71,8 @@
     class_u = np.minimum(class_line // SPREAD, SPREAD - 1)
     class_v = class_line % SPREAD
     sep_line = np.arange(2 * SPREAD - 1)
-    pick_u = (class_u[:, None] - class_u[None, :] + SPREAD - 1).reshape(-1, 1) == sep_line
-    pick_v = (class_v[:, None] - class_v[None, :] + SPREAD - 1).reshape(-1, 1) == sep_line
+    pick_u = (class_u[None, :] - class_u[:, None] + SPREAD - 1).reshape(-1, 1) == sep_line
+    pick_v = (class_v[None, :] - class_v[:, None] + SPREAD - 1).reshape(-1, 1) == sep_line
     weights = jnp.stack([separation_table(f, divisor, kernel_table) for f in frequencies])
     over_r = np.kron(np.eye(PATCH), np.ones((1, PATCH))).astype(np.float32)
     over_t = np.kron(np.ones((1, PATCH)), np.eye(PATCH)).astype(np.float32)
@@ -89,23 +89,21 @@
     spec_count = samples // frame_len
     step = 128 // math.gcd(128, frame_len)
     chunks = spec_count // step
-    flat = voltages.reshape(stn_local * pol_count, samples)
-    earlier = shifted(flat[:, samples - tap_count * frame_len :], "grid", 1)
-    extended = jnp.concatenate([earlier, flat], axis=1)
+    flat = jnp.transpose(voltages, (1, 0, 2))
+    earlier = shifted(flat[:, :, samples - tap_count * frame_len :], "grid", 1)
+    extended = jnp.concatenate([earlier, flat], axis=2)
     width = step * frame_len
     reach = (step + tap_count) * frame_len
     blocks = jnp.stack(
-        [extended[:, c * width : c * width + reach] for c in range(chunks)], axis=1
+        [extended[:, :, c * width : c * width + reach] for c in range(chunks)], axis=1
     )
     matrix = fused_filter(pfb_coeffs, dft_table(frame_len), step)
     spectra = jnp.einsum(
-        "rcm,mn->nrc", blocks, matrix, preferred_element_type=jnp.float32
+        "pcsm,mn->npcs", blocks, matrix, preferred_element_type=jnp.float32
     ).astype(jnp.bfloat16)
-    spectra = spectra.reshape(frame_len // 2, 2, step, stn_local, pol_count * chunks)
-    spectra = jnp.transpose(spectra, (0, 1, 3, 2, 4)).reshape(
-        frame_len // 2, 2, stn_local, step * pol_count * chunks
-    )
-    turned = lax.all_to_all(spectra, "stn", split_axis=0, concat_axis=2, tiled=True)
+    spectra = spectra.reshape(frame_len // 2, 2, step * pol_count * chunks, stn_local)
+    turned = lax.all_to_all(spectra, "stn", split_axis=0, concat_axis=3, tiled=True)
+    turned = jnp.transpose(turned, (0, 1, 3, 2))
     ch_dev, _, stations, depth = turned.shape
     tiles = stations // TILE
     divisor = frame_len - 1
@@ -128,7 +126,7 @@
         return jnp.stack([partner, turned_partner], axis=1), partner
 
     left, right = stacked(summed)
-    cross = jnp.einsum("ceaqk,cbsk->ceabqs", left, right, preferred_element_type=jnp.float32)
+    cross = jnp.einsum("ceaqk,cbsk->ceabsq", left, right, preferred_element_type=jnp.float32)
     joint = joint_weights([first_chan + i for i in range(ch_dev)], divisor, kernel_table)
     joint = joint * norm_factor
     patch = jnp.einsum(
@@ -142,7 +140,7 @@
     line = np.arange(TILE)
     own = jnp.where(jnp.asarray(line[:, None] < line[None, :]), own, 0.0)
     own = jnp.einsum("aiq,ceaij->ceaqj", hot_full, own, precision=high)
-    own = jnp.einsum("ceaqj,ajs->ceaqs", own, hot_full, precision=high)
+    own = jnp.einsum("ceaqj,ajs->ceasq", own, hot_full, precision=high)
     own_patch = jnp.einsum(
         "ceam,cmn->cean", own.reshape(ch_dev, 2, tiles, CLASSES * CLASSES), joint, precision=high
     )

time: 230 us -> 158 us (0.69)
  local copies, waits for them, and re-layouts: 113 us -> 41.9 us
    transpose x3 -> x0, local copies, waits for them, and re-layouts: 58.5 us -> none  [the longest x1 30.5 us: body(): jnp.transpose(spectra, (0, 1, 3, 2, 4))]
    reshape x3 -> x1, local copies, waits for them, and re-layouts: 19.4 us -> 1.42 us  [body(): spectra.reshape(frame_len // 2, 2, step * pol_count * chunks, stn_local)]
    reshape x1 -> x2, local copies, waits for them, and re-layouts: 8.38 us -> 11.2 us  [body(): patch = patch.reshape(ch_dev, 2, tiles * tiles, PATCH, PATCH)]
  transfers between devices with their start and end apart: 3 -> 3, of which waited for: 2 -> 2; matrix products, arithmetic and copies ran while one was open for 8% -> 12% of each run, Pallas kernels for 0% -> 0%
where the time goes in v1:
time: 158 us; the launch traced here: 157 us
  matrix products  51.7 us (33%)
  local copies, waits for them, and re-layouts  41.9 us (27%)
  waiting for transfers between devices  30 us (19%)
  between operations  13.9 us (9%)
  other arithmetic  10.3 us (7%)
  starting transfers between devices  9.2 us (6%)
    reshape x1, local copies, waits for them, and re-layouts, body(): cross.reshape(ch_dev, 2, tiles, tiles, CLASSES * CLASSES)  20 us
    reduce_scatter x1, waiting for transfers between devices, body(): return lax.psum_scatter(planes, 'grid', scatter_dimension=0, tiled=True)  19.1 us
    reshape x2, local copies, waits for them, and re-layouts, body(): patch = patch.reshape(ch_dev, 2, tiles * tiles, PATCH, PATCH)  11.2 us
    all_to_all x1, waiting for transfers between devices, body(): lax.all_to_all(spectra, 'stn', split_axis=0, concat_axis=3, tiled=True)  10.8 us
    dot_general x1, matrix products, body(): jnp.einsum('ceaqk,cbsk->ceabsq', left, right, preferred_element_type=jnp....  10.1 us
    dot_general x1, matrix products, body(): planes = jnp.einsum('ckru,ckrew->ucew', rows, spread_cols, precision=high)  9.85 us
    dot_general x1, matrix products, body(): spread_cols = jnp.einsum('cekrt,cktw->ckrew', patch, cols, precision=high)  9.31 us
    all_to_all x1, starting transfers between devices, body(): lax.all_to_all(spectra, 'stn', split_axis=0, concat_axis=3, tiled=True)  6.8 us
  transfers between devices with their start and end apart: 3, of which 2 were waited for; matrix products, arithmetic and copies ran while one was open for 12% of the time, Pallas kernels for 0%

profile of v1, /device:TPU:0, one launch (start us, length us, event | category | flops | bytes accessed | tf_op | source)
XLA Modules:
  0.0 157.1 jit_solution(12162237454141084076)
XLA Ops:
  6.5 1.3 copy.179
  7.9 2.4 %collective-permute-start = (bf16[2,64,768]{2,1,0:T(8,128)(2,1)S(1)}, bf16[2,64,768]{2,1,0:T(8,128)(2,1)S(1)}, u32[]{:S(2)}, u32[]{:S(2)}) collective-permute-start(bf16[2,64,768]{2,1,0:T(8,128)(2,1)S(1)} %slice.161), channel_id=1, source_target_pairs={{0,1},{1,2},{2,3},{4,5},{5,6},{6,7},{8,9},{9,10},{10,11},{12,13},{... | collective-permute-start | bytes 589832 | tf_op jit(solution)/shard_map/ppermute | solution.py:21
  10.3 0.1 multiply_convert_fusion
  10.4 0.0 copy-done.9
  10.4 0.1 reshape.1047
  10.5 0.1 fusion.102
  10.6 0.1 copy.111
  10.8 0.2 fusion.84
  11.0 0.2 fusion.85
  11.3 0.2 fusion.86
  11.5 0.0 copy-done.11
  11.5 0.1 select_add_fusion.2
  11.6 0.1 select_add_fusion.1
  11.7 0.0 copy-start.13
  11.7 0.0 copy-start.14
  11.7 0.0 copy-start.15
  11.7 0.0 copy-start.16
  11.7 0.0 copy-start.17
  11.7 0.0 copy-start.18
  11.7 0.0 copy-start.19
  11.8 0.0 copy-start.20
  11.8 0.1 select_add_fusion
  11.9 0.0 copy-done.8
  11.9 0.2 fusion.57
  12.1 0.0 copy-start.7
  12.1 4.3 %fusion.103 = f32[3,256,1024]{2,1,0:T(8,128)} fusion(f32[3,9,256]{2,1,0:T(8,128)S(1)} %fusion.57, f32[1024,9,1]{0,1,2:T(8,128)S(1)} %copy-done.6), kind=kOutput, calls=%fused_computation.179 | convolution fusion | flops 84934656 | bytes 3210240 | tf_op jit(solution)/shard_map/qz,czm->cqm/dot_general | solution.py:81
  16.4 0.2 fusion.31
  16.6 1.3 fusion.8
  18.0 0.2 fusion.56
  18.1 0.0 collective-permute-done
  18.4 1.5 convolution_convert_fusion.1
  19.9 1.3 copy.120
  21.2 0.0 copy-start.12
  21.2 1.4 copy.121
  22.6 6.8 %all-to-all-start = ((bf16[24,2,128,64]{2,3,1,0:T(8,128)(2,1)}), bf16[24,2,128,64]{2,3,1,0:T(8,128)(2,1)}, u32[]{:S(2)}, u32[]{:S(2)}) async-start(bf16[24,2,128,64]{2,3,1,0:T(8,128)(2,1)} %copy.121), calls=%async_computation | async-start | bytes 1572864 | tf_op jit(solution)/shard_map/all_to_all | solution.py:105
  29.4 0.0 reduce-scatter.2.cloned.1.call-start
  29.5 0.1 add.327
  29.6 0.3 iota_add_fusion
  29.9 4.7 %multiply_multiply_fusion = f32[3,256,1024]{2,1,0:T(8,128)S(1)} fusion(f32[3,256,1024]{2,1,0:T(8,128)} %fusion.103, f32[3,9,256]{2,1,0:T(8,128)S(1)} %fusion.56, f32[1024,9,1]{0,1,2:T(8,128)S(1)} %copy-done.5), kind=kOutput, calls=%fused_computation.12 | convolution fusion | flops 86507520 | bytes 6355968 | tf_op jit(solution)/shard_map/qz,czm->cqm/dot_general | solution.py:82
  34.6 5.6 %iota_compare_fusion = pred[3,2,256,16,128]{4,3,2,0,1:T(8,128)(4,1)} fusion(s32[3,2,256,16]{3,2,0,1:T(8,128)S(1)} %iota_add_fusion), kind=kLoop, calls=%fused_computation.2 | loop fusion | flops 3145728 | bytes 3244032 | tf_op jit(solution)/shard_map/eq | solution.py:161
  40.2 10.8 %all-to-all-done = bf16[24,2,128,64]{2,3,1,0:T(8,128)(2,1)} async-done(((bf16[24,2,128,64]{2,3,1,0:T(8,128)(2,1)}), bf16[24,2,128,64]{2,3,1,0:T(8,128)(2,1)}, u32[]{:S(2)}, u32[]{:S(2)}) %all-to-all-start) | async-done | bytes 786464 | tf_op jit(solution)/shard_map/all_to_all | solution.py:105
  51.0 1.2 copy.122
  52.2 0.1 slice_bitcast_fusion.7
  52.3 0.1 fusion.100
  52.4 0.4 fusion.28
  52.7 0.8 slice_bitcast_fusion.5
  53.5 0.8 fusion.101
  54.3 0.2 fusion.38
  54.6 1.3 bitcast_select_fusion
  55.9 0.6 fusion.16
  56.5 1.7 %fusion.18 = f32[3,2,16,32,32]{4,3,1,0,2:T(8,128)} fusion(f32[16,3,2,32,32]{4,3,2,1,0:T(8,128)S(1)} %fusion.16, s32[16,32]{1,0:T(8,128)S(1)} %add.327), kind=kOutput, calls=%fused_computation.33 | convolution fusion | flops 18890752 | bytes 788480 | tf_op jit(solution)/shard_map/ceaqj,ajs->ceasq/dot_general | solution.py:143
  58.2 3.0 %reshape.1050 = f32[3,2,16,1024]{3,1,0,2:T(2,128)} reshape(f32[3,2,16,32,32]{4,3,1,0,2:T(8,128)} %fusion.18) | data formatting | bytes 786432 | tf_op jit(solution)/shard_map/reshape | solution.py:145
  61.2 1.6 %fusion.36 = (bf16[3,16,32,256,1,1]{3,2,0,1,5,4:T(8,128)(2,1)S(1)}, bf16[3,1,16,32,256]{4,3,0,2,1:T(8,128)(2,1)S(1)}, bf16[3,1,16,32,256]{4,3,0,2,1:T(8,128)(2,1)S(1)}) fusion(bf16[3,16,32,128]{3,2,0,1:T(8,128)(2,1)} %get-tuple-element.10, bf16[3,16,32,128]{3,2,0,1:T(8,128)(2,1)S(1)} %get-tuple-element.9, bf16[3,16,32,128]{3,2,0,1:T(8,128)(2,1)} %fusion.101), kind=kLoop, calls=%fused_computation.52 | loop fusion | flops 3145728 | bytes 3538944 | tf_op jit(solution)/shard_map/concatenate | solution.py:124
  62.8 10.1 %convolution_bitcast_fusion = f32[3,2,16,16,32,32]{5,4,2,1,3,0:T(8,128)} fusion(bf16[3,16,32,256,1,1]{3,2,0,1,5,4:T(8,128)(2,1)S(1)} %get-tuple-element.7, bf16[3,1,16,32,256]{4,3,0,2,1:T(8,128)(2,1)S(1)} %get-tuple-element.13, bf16[3,1,16,32,256]{4,3,0,2,1:T(8,128)(2,1)S(1)} %get-tuple-element.8), kind=kOutput, calls=%fused_computation.3 | convolution fusion | flops 806092800 | bytes 8650752 | tf_op jit(solution)/shard_map/ceaqk,cbsk->ceabsq/dot_general | solution.py:129
  72.9 20.0 %reshape.1051 = f32[3,2,16,16,1024]{4,2,1,3,0:T(8,128)} reshape(f32[3,2,16,16,32,32]{5,4,2,1,3,0:T(8,128)} %convolution_bitcast_fusion) | data formatting | bytes 12582912 | tf_op jit(solution)/shard_map/reshape | solution.py:134
  92.9 1.5 fusion.6
  94.4 5.4 %fusion.23 = f32[3,2,16,16,256]{4,2,3,1,0:T(8,128)S(1)} fusion(f32[3,256,1024]{2,1,0:T(8,128)S(1)} %multiply_multiply_fusion, f32[3,2,16,16,1024]{4,2,1,3,0:T(8,128)} %reshape.1051, f32[3,2,16,256]{3,2,1,0:T(8,128)S(1)} %fusion.6, pred[16,16]{0,1:T(8,128)(4,1)S(1)} %copy-done.10), kind=kOutput, calls=%fused_computation.34 | convolution fusion | flops 2416312320 | bytes 11108608 | tf_op jit(solution)/shard_map/ceabm,cmn->ceabn/dot_general | solution.py:132
  99.8 2.4 %copy.157 = f32[3,2,16,16,256]{4,1,3,2,0:T(2,128)} copy(f32[3,2,16,16,256]{4,2,3,1,0:T(8,128)S(1)} %fusion.23) | data formatting | bytes 3145728 | tf_op jit(solution)/shard_map/reshape | solution.py:158
  102.1 8.9 %reshape.1095 = f32[3,2,256,16,16]{4,3,1,2,0:T(8,128)} reshape(f32[3,2,16,16,256]{4,1,3,2,0:T(2,128)} %copy.157) | data formatting | bytes 3145728 | tf_op jit(solution)/shard_map/reshape | solution.py:158
  111.0 9.3 %fusion.4 = f32[3,256,128,2,16]{2,4,3,1,0:T(8,128)} fusion(f32[3,2,256,16,16]{4,3,1,2,0:T(8,128)} %reshape.1095, pred[3,2,256,16,128]{4,3,2,0,1:T(8,128)(4,1)S(1)} %copy-done.2), kind=kOutput, calls=%fused_computation.8 | convolution fusion | flops 301989888 | bytes 15728640 | tf_op jit(solution)/shard_map/cekrt,cktw->ckrew/dot_general | solution.py:163
  120.3 9.8 %fusion = f32[3,2,128,128,1]{3,2,1,4,0:T(8,128)S(1)} fusion(f32[3,256,128,2,16]{2,4,3,1,0:T(8,128)} %fusion.4, pred[3,2,256,16,128]{4,3,2,0,1:T(8,128)(4,1)S(1)} %copy-done.2), kind=kOutput, calls=%fused_computation | convolution fusion | flops 2415919104 | bytes 14548992 | tf_op jit(solution)/shard_map/ckru,ckrew->ucew/dot_general | solution.py:164
  130.2 0.9 copy.138
  131.1 0.0 reduce-scatter.2.cloned.1.call-update
  131.1 19.1 %reduce-scatter.2.cloned.1.call-done = f32[32,3,256]{2,0,1:T(8,128)} async-done(((f32[128,3,256]{2,0,1:T(8,128)}), f32[32,3,256]{2,0,1:T(8,128)}) %reduce-scatter.2.cloned.1.call-update) | async-done | bytes 98320 | tf_op jit(solution)/shard_map/reduce_scatter | solution.py:166
  (53 shorter events, 0.5 us)
Async XLA Ops:
  6.5 4.2 %copy-start = (f32[8,7]{1,0:T(8,128)S(1)}, f32[8,7]{1,0:T(8,128)}, u32[]{:S(2)}) copy-start(f32[8,7]{1,0:T(8,128)} %param.18) | copy-start | bytes 676
  6.5 5.3 %copy-start.8 = (f32[16,256,1]{1,0,2:T(8,128)S(1)}, f32[16,256,1]{1,0,2:T(8,128)}, u32[]{:S(2)}) copy-start(f32[16,256,1]{1,0,2:T(8,128)} %constant.175) | copy-start | bytes 49156
  6.5 5.5 %copy-start.6 = (f32[1024,9,1]{0,1,2:T(8,128)S(1)}, f32[1024,9,1]{0,1,2:T(8,128)}, u32[]{:S(2)}) copy-start(f32[1024,9,1]{0,1,2:T(8,128)} %constant.176) | copy-start | bytes 110596
  6.5 3.8 %copy-start.9 = (f32[16,48]{1,0:T(8,128)S(1)}, f32[16,48]{1,0:T(8,128)}, u32[]{:S(2)}) copy-start(f32[16,48]{1,0:T(8,128)} %param.15) | copy-start | bytes 9220
  6.5 4.9 %copy-start.11 = (s32[3,2,136]{2,1,0:T(2,128)S(1)}, s32[3,2,136]{2,1,0:T(2,128)}, u32[]{:S(2)}) copy-start(s32[3,2,136]{2,1,0:T(2,128)} %param.17) | copy-start | bytes 9796
  7.9 10.2 %collective-permute-start = (bf16[2,64,768]{2,1,0:T(8,128)(2,1)S(1)}, bf16[2,64,768]{2,1,0:T(8,128)(2,1)S(1)}, u32[]{:S(2)}, u32[]{:S(2)}) collective-permute-start(bf16[2,64,768]{2,1,0:T(8,128)(2,1)S(1)} %slice.161), channel_id=1, source_target_pairs={{0,1},{1,2},{2,3},{4,5},{5,6},{6,7},{8,9},{9,10},{10,11},{12,13},{... | collective-permute-start | bytes 589832 | tf_op jit(solution)/shard_map/ppermute | solution.py:21
  11.2 5.2 %copy-start.4 = (f32[136,256,1]{1,0,2:T(8,128)S(1)}, f32[136,256,1]{1,0,2:T(8,128)}, u32[]{:S(2)}) copy-start(f32[136,256,1]{1,0,2:T(8,128)} %constant.174) | copy-start | bytes 417796
  11.2 5.2 %copy-start.21 = (s32[256]{0:T(256)S(1)}, s32[256]{0:T(256)}, u32[]{:S(2)}) copy-start(s32[256]{0:T(256)} %constant.139.clone) | copy-start | bytes 3076
  11.7 4.9 %copy-start.13 = (f32[384]{0:T(512)S(1)}, f32[384]{0:T(512)}, u32[]{:S(2)}) copy-start(f32[384]{0:T(512)} %constant.159) | copy-start | bytes 4612
  11.7 4.9 %copy-start.14 = (f32[384]{0:T(512)S(1)}, f32[384]{0:T(512)}, u32[]{:S(2)}) copy-start(f32[384]{0:T(512)} %constant.161) | copy-start | bytes 4612
  11.7 4.9 %copy-start.15 = (f32[384]{0:T(512)S(1)}, f32[384]{0:T(512)}, u32[]{:S(2)}) copy-start(f32[384]{0:T(512)} %constant.163) | copy-start | bytes 4612
  11.7 4.9 %copy-start.16 = (f32[384]{0:T(512)S(1)}, f32[384]{0:T(512)}, u32[]{:S(2)}) copy-start(f32[384]{0:T(512)} %constant.165) | copy-start | bytes 4612
  11.7 4.9 %copy-start.17 = (f32[384]{0:T(512)S(1)}, f32[384]{0:T(512)}, u32[]{:S(2)}) copy-start(f32[384]{0:T(512)} %constant.167) | copy-start | bytes 4612
  11.7 4.9 %copy-start.18 = (f32[384]{0:T(512)S(1)}, f32[384]{0:T(512)}, u32[]{:S(2)}) copy-start(f32[384]{0:T(512)} %constant.169) | copy-start | bytes 4612
  11.7 4.9 %copy-start.19 = (f32[384]{0:T(512)S(1)}, f32[384]{0:T(512)}, u32[]{:S(2)}) copy-start(f32[384]{0:T(512)} %constant.171) | copy-start | bytes 4612
  11.8 4.9 %copy-start.20 = (f32[384]{0:T(512)S(1)}, f32[384]{0:T(512)}, u32[]{:S(2)}) copy-start(f32[384]{0:T(512)} %constant.173) | copy-start | bytes 4612
  12.1 5.9 %copy-start.7 = (f32[16,256,1]{1,0,2:T(8,128)S(1)}, f32[16,256,1]{1,0,2:T(8,128)}, u32[]{:S(2)}) copy-start(f32[16,256,1]{1,0,2:T(8,128)} %constant.177) | copy-start | bytes 49156
  21.2 8.3 %copy-start.12 = (s32[2,512]{1,0:T(2,128)S(1)}, s32[2,512]{1,0:T(2,128)}, u32[]{:S(2)}) copy-start(s32[2,512]{1,0:T(2,128)} %param.16) | copy-start | bytes 12292
  22.6 7.2 %copy-start.5 = (f32[1024,9,1]{0,1,2:T(8,128)S(1)}, f32[1024,9,1]{0,1,2:T(8,128)}, u32[]{:S(2)}) copy-start(f32[1024,9,1]{0,1,2:T(8,128)} %constant.178) | copy-start | bytes 110596
  22.6 28.4 %all-to-all-start = ((bf16[24,2,128,64]{2,3,1,0:T(8,128)(2,1)}), bf16[24,2,128,64]{2,3,1,0:T(8,128)(2,1)}, u32[]{:S(2)}, u32[]{:S(2)}) async-start(bf16[24,2,128,64]{2,3,1,0:T(8,128)(2,1)} %copy.121), calls=%async_computation | async-start | bytes 1572864 | tf_op jit(solution)/shard_map/all_to_all | solution.py:105
  29.4 120.8 %reduce-scatter.2.cloned.1.call-start = ((), (), s32[]{:S(2)}) async-start(), calls=%async_computation.2 | async-start | bytes 491520 | tf_op jit(solution)/shard_map/reduce_scatter | solution.py:166
  53.5 1.0 copy-start.22
  72.9 20.0 %copy-start.3 = (f32[3,2,16,1024]{3,1,0,2:T(2,128)S(1)}, f32[3,2,16,1024]{3,1,0,2:T(2,128)}, u32[]{:S(2)}) copy-start(f32[3,2,16,1024]{3,1,0,2:T(2,128)} %reshape.1050) | copy-start | bytes 1179652
  92.9 1.5 copy-start.10
  102.1 8.9 %copy-start.2 = (pred[3,2,256,16,128]{4,3,2,0,1:T(8,128)(4,1)S(1)}, pred[3,2,256,16,128]{4,3,2,0,1:T(8,128)(4,1)}, u32[]{:S(2)}) copy-start(pred[3,2,256,16,128]{4,3,2,0,1:T(8,128)(4,1)} %iota_compare_fusion) | copy-start | bytes 9437188
  120.3 29.9 %copy-start.1 = (f32[8,7]{1,0:T(8,128)S(1)}, f32[8,7]{1,0:T(8,128)}, u32[]{:S(2)}) copy-start(f32[8,7]{1,0:T(8,128)} %param.18) | copy-start | bytes 676
Sparse Core Ops, SparseCore 0:
  131.3 18.9 reduce-scatter.1
